TPU v7x, 32 devices: a whole 2x2x4 slice. The times are simulated.
32 devices in a mesh: req: 4 (over z), exp: 8 (over y, x, core).
Axes of the slice: x: 2, y: 2, z: 4, core: 2. Of those that a mesh axis runs over, the one named last changes fastest.
Arguments:
- hidden: bfloat16 [4096, 2048], P(('req', 'exp')), may hold values from -6 to 6
- attn_gain: float32 [2048], replicated, may hold values from 0.5 to 1.5
- w_query: bfloat16 [2048, 1024], P(None, 'exp'), may hold values from -0.125 to 0.125
- w_keyval: bfloat16 [2, 2048, 1024], P(None, None, 'exp'), may hold values from -0.3125 to 0.3125
- k_pool: bfloat16 [640, 128, 1024], P('req', None, 'exp'), may hold values from -86 to 86
- v_pool: bfloat16 [640, 128, 1024], P('req', None, 'exp'), may hold values from -16 to 16
- dec_len: int32 [16], P('req'), may hold values from 1 to 4096, as said below
- dec_pages: int32 [16, 32], P('req'), may hold values from 0 to 159, as said below
- pre_pos: int32 [4], P('req'), may hold values from 0 to 4096, as said below
- pre_pages: int32 [4, 32], P('req'), may hold values from 0 to 159
- w_out: bfloat16 [1024, 2048], P('exp'), may hold values from -0.1875 to 0.1875
- moe_gain: float32 [2048], replicated, may hold values from 0.1 to 1.9
- expert_ids: int32 [4096, 8], P(('req', 'exp')), may hold values from 0 to 15, all different within a row; in each aligned block of 128 rows (0 to 127, 128 to 255, ...) at most 80 rows name the same one
- router_logits: float32 [4096, 8], P(('req', 'exp')), may hold values from -0.4 to 283
- w_in: bfloat16 [32, 2048, 1024], P(('req', 'exp')), may hold values from -0.125 to 0.125
- w_down: bfloat16 [32, 512, 2048], P(('req', 'exp')), may hold values from -0.25 to 0.25
Outputs:
- mixed: bfloat16 [4096, 2048], P(('req', 'exp'))
- new_kv: bfloat16 [2, 4096, 1024], P(None, 'req', 'exp')
Inputs may be any that keep to these rules, and one draw needn't show every extreme that they name: Within each group, the rows of dec_pages of its 4 requests and its row of pre_pages name every one of the group's 160 pages exactly once. `dec_len`: some request has exactly 4096 cached positions. `pre_pos`: some group's prefix has exactly 4096 positions. `expert_ids`: each row names 8 different experts; among the rows of one device no expert is named by more than 80 rows.
All inputs are finite; a program needn't handle non-finite values.
Results may differ from a plain program's by a relative error of at most 0.02.
Values may be sent and summed in bfloat16 or wider, within the bound.
No kernel may reach another device: no remote copies, remote signals or barrier semaphores. Data moves between devices by JAX's collectives and lax.ppermute only.
A program may use at most 128 MiB of HBM per device.

v0:
```python
import math

import jax
import jax.numpy as jnp
from jax import lax
from jax.sharding import PartitionSpec as P

HD = 128
SPLIT = 2


EPSILON = 1e-05
THETA = 10000.0


def rms_scale(inputs, gain):
    values = inputs.astype(jnp.float32)
    mean_square = jnp.mean(values * values, axis=-1, keepdims=True)
    return (values * lax.rsqrt(mean_square + EPSILON) * gain).astype(jnp.bfloat16)


def rotate(values, positions):
    head_size = values.shape[-1]
    half = head_size // 2
    steps = jnp.arange(half, dtype=jnp.float32)
    frequency = jnp.exp(steps * (-2.0 * math.log(THETA) / head_size))
    angles = positions.astype(jnp.float32)[:, None, None] * frequency[None, None, :]
    cosine = jnp.cos(angles)
    sine = jnp.sin(angles)
    first = values[..., :half]
    second = values[..., half:]
    return jnp.concatenate(
        [first * cosine - second * sine, second * cosine + first * sine], axis=-1
    )


def online_block(state, query, keys, values, allowed, scale):
    old_max, old_total, running = state
    scores = jnp.einsum("qd,kd->qk", query, keys, preferred_element_type=jnp.float32) * scale
    scores = jnp.where(allowed, scores, -jnp.inf)
    new_max = jnp.maximum(old_max, jnp.max(scores, axis=1))
    anchor = jnp.where(jnp.isfinite(new_max), new_max, 0.0)
    shrink = jnp.exp(old_max - anchor)
    weights = jnp.exp(scores - anchor[:, None])
    new_total = old_total * shrink + jnp.sum(weights, axis=1)
    running = running * shrink[:, None] + jnp.dot(
        weights.astype(jnp.bfloat16), values, preferred_element_type=jnp.float32
    )
    return (new_max, new_total, running)


def deliver(buffer):
    result = lax.all_to_all(buffer, ("req", "exp"), split_axis=0, concat_axis=0, tiled=True)
    return result


def bring_back(buffer):
    result = lax.all_to_all(buffer, ("req", "exp"), split_axis=0, concat_axis=0, tiled=True)
    return result


def body(
    hidden,
    attn_gain,
    w_query,
    w_keyval,
    k_pool,
    v_pool,
    dec_len,
    dec_pages,
    pre_pos,
    pre_pages,
    w_out,
    moe_gain,
    expert_ids,
    router_logits,
    w_in,
    w_down,
):
    local_rows, width = hidden.shape
    req_count = lax.axis_size("req")
    exp_count = lax.axis_size("exp")
    devices = req_count * exp_count
    group_rows = local_rows * exp_count
    dec_count = dec_len.shape[0]
    segment = group_rows - dec_count
    local_width = w_query.shape[1]
    heads_here = local_width // HD
    page_size = k_pool.shape[1]
    scale = 1.0 / math.sqrt(HD)
    normed_attn = rms_scale(hidden, attn_gain)
    joined = jnp.concatenate([w_query, w_keyval[0], w_keyval[1]], axis=1)
    projected_rows = jnp.dot(
        lax.all_gather(normed_attn, "exp", axis=0, tiled=True),
        joined,
        preferred_element_type=jnp.float32,
    )
    row_index = jnp.arange(group_rows, dtype=jnp.int32)
    dec_index = jnp.minimum(row_index, dec_count - 1)
    positions = jnp.where(
        row_index < dec_count, dec_len[dec_index], pre_pos[0] + row_index - dec_count
    )
    query = rotate(
        projected_rows[:, :local_width].reshape(group_rows, heads_here, HD), positions
    ).astype(jnp.bfloat16)
    keys_new = rotate(
        projected_rows[:, local_width : 2 * local_width].reshape(group_rows, heads_here, HD),
        positions,
    ).astype(jnp.bfloat16)
    values_new = (
        projected_rows[:, 2 * local_width :]
        .reshape(group_rows, heads_here, HD)
        .astype(jnp.bfloat16)
    )
    new_kv = jnp.stack(
        [keys_new.reshape(group_rows, local_width), values_new.reshape(group_rows, local_width)]
    )
    cache_len = dec_pages.shape[1] * page_size
    table_keys = k_pool[dec_pages].reshape(dec_count, cache_len, heads_here, HD)
    table_values = v_pool[dec_pages].reshape(dec_count, cache_len, heads_here, HD)
    dec_query = query[:dec_count]
    dec_scores = (
        jnp.einsum("rhd,rkhd->rhk", dec_query, table_keys, preferred_element_type=jnp.float32)
        * scale
    )
    own_score = (
        jnp.einsum(
            "rhd,rhd->rh", dec_query, keys_new[:dec_count], preferred_element_type=jnp.float32
        )
        * scale
    )
    visible = (jnp.arange(cache_len, dtype=jnp.int32)[None, :] < dec_len[:, None])[:, None, :]
    dec_scores = jnp.where(visible, dec_scores, -jnp.inf)
    highest = jnp.maximum(jnp.max(dec_scores, axis=2), own_score)
    dec_weights = jnp.exp(dec_scores - highest[..., None])
    own_weight = jnp.exp(own_score - highest)
    dec_total = jnp.sum(dec_weights, axis=2) + own_weight
    own_rounded = lax.optimization_barrier(own_weight.astype(jnp.bfloat16)).astype(jnp.float32)
    dec_summed = jnp.einsum(
        "rhk,rkhd->rhd",
        dec_weights.astype(jnp.bfloat16),
        table_values,
        preferred_element_type=jnp.float32,
    )
    dec_summed = dec_summed + own_rounded[..., None] * values_new[:dec_count].astype(jnp.float32)
    dec_out = (
        (dec_summed / dec_total[..., None]).astype(jnp.bfloat16).reshape(dec_count, local_width)
    )
    prefix_count = pre_pages.shape[1]
    block_pages = math.gcd(prefix_count, max(1, 512 // page_size))
    block_keys = block_pages * page_size
    block_count = prefix_count // block_pages
    length = pre_pos[0]
    order = jnp.arange(segment, dtype=jnp.int32)
    causal = order[None, :] <= order[:, None]
    seg_query = query[dec_count:, 0]

    def prefix_step(block, state):
        chosen = lax.dynamic_slice_in_dim(pre_pages[0], block * block_pages, block_pages)
        block_k = k_pool[chosen].reshape(block_keys, HD)
        block_v = v_pool[chosen].reshape(block_keys, HD)
        slots = block * block_keys + jnp.arange(block_keys, dtype=jnp.int32)
        return online_block(state, seg_query, block_k, block_v, (slots < length)[None, :], scale)

    start_state = (
        jnp.full((segment,), -jnp.inf, jnp.float32),
        jnp.zeros((segment,), jnp.float32),
        jnp.zeros((segment, HD), jnp.float32),
    )
    state = lax.fori_loop(0, block_count, prefix_step, start_state)
    state = online_block(
        state, seg_query, keys_new[dec_count:, 0], values_new[dec_count:, 0], causal, scale
    )
    head_outputs = (state[2] / state[1][:, None]).astype(jnp.bfloat16)
    attended = jnp.concatenate([dec_out, head_outputs], axis=0)
    projected = lax.psum_scatter(
        jnp.dot(attended, w_out, preferred_element_type=jnp.float32).astype(jnp.bfloat16),
        "exp",
        scatter_dimension=0,
        tiled=True,
    ).astype(jnp.float32)
    residual = (hidden.astype(jnp.float32) + projected).astype(jnp.bfloat16)
    normed_moe = rms_scale(residual, moe_gain)
    gates = jax.nn.softmax(router_logits, axis=-1)
    experts = devices // SPLIT
    top = expert_ids.shape[1]
    capacity = 2 * ((local_rows * top * 5 + 8 * experts - 1) // (8 * experts))
    assigned = expert_ids.reshape(-1)
    count_all = assigned.shape[0]
    marks = (assigned[:, None] == jnp.arange(experts, dtype=jnp.int32)[None, :]).astype(jnp.int32)
    earlier = jnp.cumsum(marks, axis=0) - marks
    place = jnp.sum(earlier * marks, axis=1)
    target = assigned * capacity + place
    owner_rows = jnp.arange(count_all, dtype=jnp.int32) // top
    outgoing = (
        jnp.zeros((experts * capacity, width), jnp.bfloat16).at[target].set(normed_moe[owner_rows])
    )
    doubled = jnp.broadcast_to(
        outgoing.reshape(experts, 1, capacity, width), (experts, SPLIT, capacity, width)
    ).reshape(devices, capacity, width)
    arrived = deliver(doubled)
    piece_units = w_down.shape[1]
    inner = jnp.dot(
        arrived.reshape(devices * capacity, width), w_in[0], preferred_element_type=jnp.float32
    )
    activated = (jax.nn.silu(inner[:, :piece_units]) * inner[:, piece_units:]).astype(jnp.bfloat16)
    partial_value = (
        jnp.dot(activated, w_down[0], preferred_element_type=jnp.float32)
        .astype(jnp.bfloat16)
        .reshape(devices, capacity, width)
    )
    returned = bring_back(partial_value).reshape(devices * capacity, width)
    base_index = assigned * (SPLIT * capacity) + place
    lower_half = returned[base_index].astype(jnp.float32)
    upper_half = returned[base_index + capacity].astype(jnp.float32)
    weighted = (lower_half + upper_half) * gates.reshape(-1)[:, None]
    moe_out = jnp.sum(weighted.reshape(local_rows, top, width), axis=1)
    mixed = (residual.astype(jnp.float32) + moe_out).astype(jnp.bfloat16)
    return (mixed, new_kv)


def solution(mesh):
    placed = (
        P(("req", "exp"), None),
        P(),
        P(None, "exp"),
        P(None, None, "exp"),
        P("req", None, "exp"),
        P("req", None, "exp"),
        P("req"),
        P("req", None),
        P("req"),
        P("req", None),
        P("exp", None),
        P(),
        P(("req", "exp"), None),
        P(("req", "exp"), None),
        P(("req", "exp"), None, None),
        P(("req", "exp"), None, None),
    )
    return jax.shard_map(
        body,
        mesh=mesh,
        in_specs=placed,
        out_specs=(P(("req", "exp"), None), P(None, "req", "exp")),
        check_vma=False,
    )
```

profile of v0, /device:TPU:0, one launch (start us, length us, event | category | flops | bytes accessed | tf_op | source)
XLA Modules:
  0.0 772.8 jit_solution(4330760329202986214)
XLA Ops:
  7.2 1.4 fusion.36
  8.6 2.0 fusion.38
  12.2 5.5 gather_fusion.3
  17.7 5.7 gather_fusion.2
  24.0 2.5 compare_select_fusion.5
  26.5 1.1 slice_bitcast_fusion.3
  27.6 22.6 %all-gather.2.cloned.1.call-done = bf16[1024,2048]{1,0:T(8,128)(2,1)} async-done(((bf16[128,2048]{1,0:T(8,128)(2,1)}), bf16[1024,2048]{1,0:T(8,128)(2,1)}) %all-gather.2.cloned.1.call-update) | async-done | bytes 4194320 | tf_op jit(solution)/shard_map/all_gather | solution.py:94
  50.2 5.8 fusion.101
  56.1 2.8 fusion.63
  59.3 2.7 fusion.20
  62.1 77.9 %while.18 = (s32[]{:T(128)}, f32[1020]{0:T(1024)S(1)}, f32[1020]{0:T(1024)S(1)}, f32[1020,128]{1,0:T(8,128)}, s32[]{:T(128)}, /*index=5*/s32[1,32]{1,0:T(1,128)S...) while((s32[]{:T(128)}, f32[1020]{0:T(1024)S(1)}, ...), condition=%wide.region_6.7_spmd.clone, body=%wide.region_3.6_spmd.clone.sunk | while | flops 273534432 | bytes 12612695 | solution.py:170
  62.8 3.1 gather_fusion.1
  65.9 3.1 gather_fusion
  72.5 3.1 gather_fusion.1
  75.6 3.1 gather_fusion
  82.3 3.1 gather_fusion.1
  85.3 3.1 gather_fusion
  89.5 1.0 convolution_add_fusion.2
  92.0 3.1 gather_fusion.1
  95.1 3.1 gather_fusion
  101.7 3.1 gather_fusion.1
  104.8 3.1 gather_fusion
  111.5 3.1 gather_fusion.1
  114.5 3.1 gather_fusion
  121.2 3.1 gather_fusion.1
  124.3 3.1 gather_fusion
  130.9 3.1 gather_fusion.1
  134.0 3.1 gather_fusion
  138.1 1.0 convolution_add_fusion.2
  139.9 3.5 fusion.88
  144.6 1.0 copy-done.4
  146.9 2.0 fusion.47
  149.0 3.2 convolution_convert_fusion.1
  152.7 4.5 reduce-window.6
  157.9 45.8 %reduce-scatter.2.cloned.1.call-done = bf16[128,2048]{1,0:T(8,128)(2,1)} async-done(((bf16[1024,2048]{1,0:T(8,128)(2,1)}), bf16[128,2048]{1,0:T(8,128)(2,1)}) %reduce-scatter.2.cloned.1.call-update) | async-done | bytes 524304 | tf_op jit(solution)/shard_map/reduce_scatter | solution.py:176
  203.7 1.3 fusion.40
  205.0 2.0 fusion.42
  207.1 23.7 %scatter_custom_fusion = bf16[1280,2048]{1,0:T(8,128)(2,1)} fusion(s32[1024]{0:T(1024)S(1)} %bitcast.136, bf16[128,2048]{1,0:T(8,128)(2,1)} %fusion.42, s32[1024]{0:T(1024)S(1)} %broadcast_clamp_fusion.2, bf16[]{:T(256)} %constant.121.clone.1), kind=kCustom, calls=%fused_computation.37 | custom fusion | bytes 5243392 | tf_op jit(solution)/shard_map/scatter | solution.py:196
  230.8 8.2 %broadcast_in_dim.114 = bf16[16,2,80,2048]{3,2,1,0:T(8,128)(2,1)} broadcast(bf16[16,80,2048]{2,1,0:T(8,128)(2,1)} %bitcast.119), dimensions={0,2,3} | broadcast | bytes 15728640 | tf_op jit(solution)/shard_map/broadcast_in_dim | solution.py:198
  239.0 233.5 %all_to_all.10 = bf16[32,80,2048]{2,1,0:T(8,128)(2,1)S(1)} all-to-all(bf16[32,80,2048]{2,1,0:T(8,128)(2,1)} %bitcast.117), channel_id=1, replica_groups=mesh['req'=4,'exp'=8] {'req','exp'}, dimensions={0} | all-to-all | bytes 20971520 | tf_op jit(solution)/shard_map/all_to_all | solution.py:53
  472.6 11.5 %fusion.14 = f32[2560,1024]{1,0:T(8,128)S(1)} fusion(bf16[2560,2048]{1,0:T(8,128)(2,1)S(1)} %bitcast.123, bf16[1,2048,1024]{2,1,0:T(8,128)(2,1)S(1)} %copy-done.11), kind=kOutput, calls=%fused_computation.35 | convolution fusion | flops 10737418240 | bytes 25165824 | tf_op jit(solution)/shard_map/dot_general | solution.py:203
  484.1 8.4 %convolution_convert_fusion = bf16[2560,2048]{1,0:T(8,128)(2,1)} fusion(f32[2560,1024]{1,0:T(8,128)S(1)} %fusion.14, bf16[1,512,2048]{2,1,0:T(8,128)(2,1)S(1)} %copy-done), kind=kOutput, calls=%fused_computation.30 | convolution fusion | flops 5381816320 | bytes 23068672 | tf_op jit(solution)/shard_map/dot_general | solution.py:208
  492.5 4.1 all-to-all-start.1
  498.7 230.2 %all-to-all-done.1 = bf16[32,80,2048]{2,1,0:T(8,128)(2,1)} async-done(((bf16[32,80,2048]{2,1,0:T(8,128)(2,1)}), bf16[32,80,2048]{2,1,0:T(8,128)(2,1)}, u32[]{:S(2)}, u32[]{:S(2)}) %all-to-all-start.1) | async-done | bytes 10485792 | tf_op jit(solution)/shard_map/all_to_all | solution.py:58
  728.9 14.1 %gather_fusion.5 = bf16[1024,2048]{1,0:T(8,128)(2,1)} fusion(bf16[2560,2048]{1,0:T(8,128)(2,1)} %bitcast.34, s32[1024]{0:T(1024)S(1)} %broadcast_clamp_fusion), kind=kCustom, calls=%fused_computation.6 | custom fusion | bytes 8392704 | tf_op jit(solution)/shard_map/gather | solution.py:215
  743.0 14.2 %gather_fusion.4 = bf16[1024,2048]{1,0:T(8,128)(2,1)} fusion(bf16[2560,2048]{1,0:T(8,128)(2,1)} %bitcast.34, s32[1024]{0:T(1024)S(1)} %broadcast_clamp_fusion.1), kind=kCustom, calls=%fused_computation.5 | custom fusion | bytes 8392704 | tf_op jit(solution)/shard_map/gather | solution.py:214
  757.2 7.6 fusion.12
  764.8 1.0 fusion.43
  (184 shorter events, 34.1 us)
Async XLA Ops:
  7.2 476.9 %copy-start = (bf16[1,512,2048]{2,1,0:T(8,128)(2,1)S(1)}, bf16[1,512,2048]{2,1,0:T(8,128)(2,1)}, u32[]{:S(2)}) copy-start(bf16[1,512,2048]{2,1,0:T(8,128)(2,1)} %param.33) | copy-start | bytes 6291460
  7.2 43.0 %all-gather.2.cloned.1.call-start = ((), (), s32[]{:S(2)}) async-start(), calls=%async_computation.3 | async-start | bytes 4718592 | tf_op jit(solution)/shard_map/all_gather | solution.py:94
  10.7 193.1 %reduce-scatter.2.cloned.1.call-start = ((), (), s32[]{:S(2)}) async-start(), calls=%async_computation.4 | async-start | bytes 4718592 | tf_op jit(solution)/shard_map/reduce_scatter | solution.py:176
  17.7 5.7 copy-start.9
  17.7 8.9 %copy-start.5 = (bf16[2,2048,128]{2,1,0:T(8,128)(2,1)S(1)}, bf16[2,2048,128]{2,1,0:T(8,128)(2,1)}, u32[]{:S(2)}) copy-start(bf16[2,2048,128]{2,1,0:T(8,128)(2,1)} %param.21) | copy-start | bytes 3145732
  58.9 3.2 copy-start.12
  68.9 1.0 copy-start.13
  71.0 0.8 copy-start.14
  78.7 1.0 copy-start.13
  80.7 0.8 copy-start.14
  88.4 1.0 copy-start.13
  90.4 0.8 copy-start.14
  98.1 1.0 copy-start.13
  100.2 0.8 copy-start.14
  107.9 1.0 copy-start.13
  109.9 0.8 copy-start.14
  117.6 1.0 copy-start.13
  119.6 0.8 copy-start.14
  127.3 1.0 copy-start.13
  129.4 0.8 copy-start.14
  137.1 1.0 copy-start.13
  139.1 0.8 copy-start.14
  139.9 4.0 copy-start.1
  143.4 2.2 copy-start.4
  143.9 3.0 copy-start.15
  146.9 2.0 copy-start.6
  148.9 3.2 copy-start.8
  152.1 51.6 %copy-start.2 = (bf16[128,2048]{1,0:T(8,128)(2,1)S(1)}, bf16[128,2048]{1,0:T(8,128)(2,1)}, u32[]{:S(2)}) copy-start(bf16[128,2048]{1,0:T(8,128)(2,1)} %param.18) | copy-start | bytes 1572868
  152.1 52.9 %copy-start.10 = (f32[2048]{0:T(1024)S(1)}, f32[2048]{0:T(1024)}, u32[]{:S(2)}) copy-start(f32[2048]{0:T(1024)} %param.29) | copy-start | bytes 24580
  239.0 233.5 %copy-start.11 = (bf16[1,2048,1024]{2,1,0:T(8,128)(2,1)S(1)}, bf16[1,2048,1024]{2,1,0:T(8,128)(2,1)}, u32[]{:S(2)}) copy-start(bf16[1,2048,1024]{2,1,0:T(8,128)(2,1)} %param.32) | copy-start | bytes 12582916
  492.5 4.1 copy-start.7
  492.5 236.4 %all-to-all-start.1 = ((bf16[32,80,2048]{2,1,0:T(8,128)(2,1)}), bf16[32,80,2048]{2,1,0:T(8,128)(2,1)}, u32[]{:S(2)}, u32[]{:S(2)}) async-start(bf16[32,80,2048]{2,1,0:T(8,128)(2,1)} %bitcast.122), calls=%async_computation.2 | async-start | bytes 20971520 | tf_op jit(solution)/shard_map/all_to_all | solution.py:58
  757.2 7.7 copy-start.3
Sparse Core Ops, SparseCore 0:
  10.8 39.4 all-gather.1
  152.3 51.3 reduce-scatter.1
where the time goes:
time: 778 us; the launch traced here: 773 us
  waiting for transfers between devices  299 us (38%)
  blocking collectives  234 us (30%)
  local copies, waits for them, and re-layouts  132 us (17%)
  matrix products  49.3 us (6%)
  other arithmetic  39.3 us (5%)
  between operations  15.2 us (2%)
    all_to_all x1, blocking collectives, deliver(): lax.all_to_all(buffer, ('req', 'exp'), split_axis=0, concat_axis=0, tiled...  234 us
    all_to_all x1, waiting for transfers between devices, bring_back(): lax.all_to_all(buffer, ('req', 'exp'), split_axis=0, concat_axis=0, tiled...  230 us
    reduce_scatter x1, waiting for transfers between devices, body(): lax.psum_scatter(jnp.dot(attended, w_out, preferred_element_type=jnp.floa...  45.8 us
    gather x8, local copies, waits for them, and re-layouts, prefix_step(): block_k = k_pool[chosen].reshape(block_keys, HD)  24.5 us
    gather x8, local copies, waits for them, and re-layouts, prefix_step(): block_v = v_pool[chosen].reshape(block_keys, HD)  24.5 us
    scatter x1, local copies, waits for them, and re-layouts, body(): jnp.zeros((experts * capacity, width), jnp.bfloat16).at[target]  23.7 us
    all_gather x1, waiting for transfers between devices, body(): lax.all_gather(normed_attn, 'exp', axis=0, tiled=True)  22.6 us
  transfers between devices with their start and end apart: 3, of which 3 were waited for; matrix products, arithmetic and copies ran while one was open for 3% of the time, Pallas kernels for 0%

commit v1 on v0

--- a/solution.py
+++ b/solution.py
@@ -49,6 +49,91 @@
     return (new_max, new_total, running)
 
 
+AXES = ("req", "exp")
+WIDE = jnp.float32
+
+
+def swap(values, bits):
+    count = lax.axis_size("exp")
+    return lax.ppermute(values, "exp", [(d, d ^ bits) for d in range(count)])
+
+
+def shift(values, steps):
+    count = lax.axis_size("req")
+    return lax.ppermute(values, "req", [(d, (d + steps) % count) for d in range(count)])
+
+
+def plane_gather(rows):
+    half = rows.shape[0] // 2
+    from_x = swap(rows, 2)
+    from_y = swap(rows, 4)
+    corner = [swap(from_x[:half], 4), swap(from_y[half:], 2)]
+    return [rows, from_x, from_y, jnp.concatenate(corner, axis=0)]
+
+
+def plane_reduce(parts):
+    own, for_x, for_y, corner = parts
+    half = own.shape[0] // 2
+    via_x = swap(corner[:half], 2)
+    via_y = swap(corner[half:], 4)
+    sum_y = (for_y[:half].astype(WIDE) + via_x.astype(WIDE)).astype(own.dtype)
+    sum_x = (for_x[half:].astype(WIDE) + via_y.astype(WIDE)).astype(own.dtype)
+    back_y = swap(jnp.concatenate([sum_y, for_y[half:]], axis=0), 4)
+    back_x = swap(jnp.concatenate([for_x[:half], sum_x], axis=0), 2)
+    return own.astype(WIDE) + back_x.astype(WIDE) + back_y.astype(WIDE)
+
+
+def dense_experts(normed_moe, gate_rows, w_in, w_down):
+    own_in, own_down = w_in[0], w_down[0]
+    pair_in, pair_down = swap(own_in, 1), swap(own_down, 1)
+    units = own_down.shape[0]
+    req_count = lax.axis_size("req")
+    slots = []
+    current = normed_moe
+    for step in range(req_count):
+        slots.append(plane_gather(current))
+        if step + 1 < req_count:
+            current = shift(current, 1)
+    partials = []
+    for step in range(req_count):
+        rows = jnp.concatenate(slots[step], axis=0)
+        total = 0.0
+        for part_in, part_down in ((own_in, own_down), (pair_in, pair_down)):
+            inner = jnp.dot(rows, part_in, preferred_element_type=WIDE)
+            activated = (jax.nn.silu(inner[:, :units]) * inner[:, units:]).astype(jnp.bfloat16)
+            total = total + jnp.dot(activated, part_down, preferred_element_type=WIDE)
+        scaled = (total * gate_rows[step][:, None]).astype(jnp.bfloat16)
+        partials.append(jnp.split(scaled, 4, axis=0))
+    result = 0.0
+    for step in list(range(1, req_count)) + [0]:
+        reduced = plane_reduce(partials[step])
+        if step:
+            reduced = shift(reduced.astype(jnp.bfloat16), -step).astype(WIDE)
+        result = result + reduced
+    return result
+
+
+def gate_table(expert_ids, gates):
+    req_count = lax.axis_size("req")
+    exp_count = lax.axis_size("exp")
+    devices = req_count * exp_count
+    experts = devices // SPLIT
+    rows = expert_ids.shape[0]
+    named = expert_ids[:, :, None] == jnp.arange(experts, dtype=jnp.int32)
+    table = jnp.sum(jnp.where(named, gates[:, :, None], 0.0), axis=1)
+    table = lax.all_gather(table, AXES, axis=0, tiled=True).reshape(devices, rows, experts)
+    group = lax.axis_index("req")
+    place = lax.axis_index("exp")
+    mine = (group * exp_count + place) // SPLIT
+    column = jnp.sum(jnp.where(jnp.arange(experts) == mine, table, 0.0), axis=-1)
+    steps = jnp.arange(req_count, dtype=jnp.int32)[:, None]
+    bits = jnp.arange(0, exp_count, 2, dtype=jnp.int32)[None, :]
+    source = ((group - steps) % req_count) * exp_count + (place ^ bits)
+    chosen = source[:, :, None] == jnp.arange(devices, dtype=jnp.int32)
+    picked = jnp.sum(jnp.where(chosen[..., None], column[None, None], 0.0), axis=2)
+    return picked.reshape(req_count, -1)
+
+
 def deliver(buffer):
     result = lax.all_to_all(buffer, ("req", "exp"), split_axis=0, concat_axis=0, tiled=True)
     return result
@@ -57,6 +142,45 @@
 def bring_back(buffer):
     result = lax.all_to_all(buffer, ("req", "exp"), split_axis=0, concat_axis=0, tiled=True)
     return result
+
+
+def sparse_experts(normed_moe, expert_ids, gates, w_in, w_down):
+    local_rows, width = normed_moe.shape
+    devices = lax.axis_size("req") * lax.axis_size("exp")
+    experts = devices // SPLIT
+    top = expert_ids.shape[1]
+    capacity = 2 * ((local_rows * top * 5 + 8 * experts - 1) // (8 * experts))
+    assigned = expert_ids.reshape(-1)
+    count_all = assigned.shape[0]
+    marks = (assigned[:, None] == jnp.arange(experts, dtype=jnp.int32)[None, :]).astype(jnp.int32)
+    earlier = jnp.cumsum(marks, axis=0) - marks
+    place = jnp.sum(earlier * marks, axis=1)
+    target = assigned * capacity + place
+    owner_rows = jnp.arange(count_all, dtype=jnp.int32) // top
+    outgoing = (
+        jnp.zeros((experts * capacity, width), jnp.bfloat16).at[target].set(normed_moe[owner_rows])
+    )
+    doubled = jnp.broadcast_to(
+        outgoing.reshape(experts, 1, capacity, width), (experts, SPLIT, capacity, width)
+    ).reshape(devices, capacity, width)
+    arrived = deliver(doubled)
+    piece_units = w_down.shape[1]
+    inner = jnp.dot(
+        arrived.reshape(devices * capacity, width), w_in[0], preferred_element_type=jnp.float32
+    )
+    activated = (jax.nn.silu(inner[:, :piece_units]) * inner[:, piece_units:]).astype(jnp.bfloat16)
+    partial_value = (
+        jnp.dot(activated, w_down[0], preferred_element_type=jnp.float32)
+        .astype(jnp.bfloat16)
+        .reshape(devices, capacity, width)
+    )
+    returned = bring_back(partial_value).reshape(devices * capacity, width)
+    base_index = assigned * (SPLIT * capacity) + place
+    lower_half = returned[base_index].astype(jnp.float32)
+    upper_half = returned[base_index + capacity].astype(jnp.float32)
+    weighted = (lower_half + upper_half) * gates.reshape(-1)[:, None]
+    moe_out = jnp.sum(weighted.reshape(local_rows, top, width), axis=1)
+    return moe_out
 
 
 def body(
@@ -182,39 +306,10 @@
     residual = (hidden.astype(jnp.float32) + projected).astype(jnp.bfloat16)
     normed_moe = rms_scale(residual, moe_gain)
     gates = jax.nn.softmax(router_logits, axis=-1)
-    experts = devices // SPLIT
-    top = expert_ids.shape[1]
-    capacity = 2 * ((local_rows * top * 5 + 8 * experts - 1) // (8 * experts))
-    assigned = expert_ids.reshape(-1)
-    count_all = assigned.shape[0]
-    marks = (assigned[:, None] == jnp.arange(experts, dtype=jnp.int32)[None, :]).astype(jnp.int32)
-    earlier = jnp.cumsum(marks, axis=0) - marks
-    place = jnp.sum(earlier * marks, axis=1)
-    target = assigned * capacity + place
-    owner_rows = jnp.arange(count_all, dtype=jnp.int32) // top
-    outgoing = (
-        jnp.zeros((experts * capacity, width), jnp.bfloat16).at[target].set(normed_moe[owner_rows])
-    )
-    doubled = jnp.broadcast_to(
-        outgoing.reshape(experts, 1, capacity, width), (experts, SPLIT, capacity, width)
-    ).reshape(devices, capacity, width)
-    arrived = deliver(doubled)
-    piece_units = w_down.shape[1]
-    inner = jnp.dot(
-        arrived.reshape(devices * capacity, width), w_in[0], preferred_element_type=jnp.float32
-    )
-    activated = (jax.nn.silu(inner[:, :piece_units]) * inner[:, piece_units:]).astype(jnp.bfloat16)
-    partial_value = (
-        jnp.dot(activated, w_down[0], preferred_element_type=jnp.float32)
-        .astype(jnp.bfloat16)
-        .reshape(devices, capacity, width)
-    )
-    returned = bring_back(partial_value).reshape(devices * capacity, width)
-    base_index = assigned * (SPLIT * capacity) + place
-    lower_half = returned[base_index].astype(jnp.float32)
-    upper_half = returned[base_index + capacity].astype(jnp.float32)
-    weighted = (lower_half + upper_half) * gates.reshape(-1)[:, None]
-    moe_out = jnp.sum(weighted.reshape(local_rows, top, width), axis=1)
+    if exp_count == 8:
+        moe_out = dense_experts(normed_moe, gate_table(expert_ids, gates), w_in, w_down)
+    else:
+        moe_out = sparse_experts(normed_moe, expert_ids, gates, w_in, w_down)
     mixed = (residual.astype(jnp.float32) + moe_out).astype(jnp.bfloat16)
     return (mixed, new_kv)
 

time: 778 us -> 421 us (0.54)
  blocking collectives: 234 us -> 41.7 us
  waiting for transfers between devices: 299 us -> 135 us
  local copies, waits for them, and re-layouts: 132 us -> 63.4 us
  starting transfers between devices: 4.16 us -> 48.4 us
  matrix products: 49.3 us -> 84.2 us
  other arithmetic: 39.3 us -> 26.9 us
    all_to_all x1 -> x0, blocking collectives: 234 us -> none  [deliver(): lax.all_to_all(buffer, ('req', 'exp'), split_axis=0, concat_axis=0, tiled...]
    all_to_all x1 -> x0, waiting for transfers between devices: 230 us -> none  [bring_back(): lax.all_to_all(buffer, ('req', 'exp'), split_axis=0, concat_axis=0, tiled...]
    ppermute x0 -> x40, waiting for transfers between devices: none -> 99.2 us  [the longest x34 68.4 us: swap(): return lax.ppermute(values, 'exp', [(d, d ^ bits) for d in range(count)])]
    ppermute x0 -> x40, starting transfers between devices: none -> 48.4 us  [the longest x34 34.3 us: swap(): return lax.ppermute(values, 'exp', [(d, d ^ bits) for d in range(count)])]
    all_gather x0 -> x1, blocking collectives: none -> 41.7 us  [gate_table(): lax.all_gather(table, AXES, axis=0, tiled=True)]
    reduce_scatter x1, waiting for transfers between devices: 45.8 us -> 11.5 us  [body(): lax.psum_scatter(jnp.dot(attended, w_out, preferred_element_type=jnp.floa...]
    gather x2 -> x0, local copies, waits for them, and re-layouts: 28.3 us -> none  [the longest x1 14.2 us: body(): lower_half = returned[base_index].astype(jnp.float32)]
    dot_general x2 -> x16, matrix products: 19.9 us -> 44.4 us  [the longest x8 27.5 us: dense_experts(): inner = jnp.dot(rows, part_in, preferred_element_type=WIDE)]
  transfers between devices with their start and end apart: 3 -> 42, of which waited for: 3 -> 21; matrix products, arithmetic and copies ran while one was open for 3% -> 16% of each run, Pallas kernels for 0% -> 0%
where the time goes in v1:
time: 421 us; the launch traced here: 416 us
  waiting for transfers between devices  135 us (32%)
  matrix products  84.2 us (20%)
  local copies, waits for them, and re-layouts  63.4 us (15%)
  starting transfers between devices  48.4 us (11%)
  blocking collectives  41.7 us (10%)
  other arithmetic  26.9 us (6%)
  between operations  15.7 us (4%)
    ppermute x34, waiting for transfers between devices, swap(): return lax.ppermute(values, 'exp', [(d, d ^ bits) for d in range(count)])  68.4 us
    all_gather x1, blocking collectives, gate_table(): lax.all_gather(table, AXES, axis=0, tiled=True)  41.7 us
    ppermute x34, starting transfers between devices, swap(): return lax.ppermute(values, 'exp', [(d, d ^ bits) for d in range(count)])  34.3 us
    ppermute x6, waiting for transfers between devices, shift(): lax.ppermute(values, 'req', [(d, (d + steps) % count) for d in range(coun...  30.8 us
    dot_general x8, matrix products, dense_experts(): inner = jnp.dot(rows, part_in, preferred_element_type=WIDE)  27.5 us
    gather x8, local copies, waits for them, and re-layouts, prefix_step(): block_v = v_pool[chosen].reshape(block_keys, HD)  24.5 us
    gather x8, local copies, waits for them, and re-layouts, prefix_step(): block_k = k_pool[chosen].reshape(block_keys, HD)  24.4 us
    all_gather x1, waiting for transfers between devices, body(): lax.all_gather(normed_attn, 'exp', axis=0, tiled=True)  24.3 us
  transfers between devices with their start and end apart: 42, of which 21 were waited for; matrix products, arithmetic and copies ran while one was open for 16% of the time, Pallas kernels for 0%

profile of v1, /device:TPU:0, one launch (start us, length us, event | category | flops | bytes accessed | tf_op | source)
XLA Modules:
  0.0 415.9 jit_solution(7343481698151306457)
XLA Ops:
  11.4 5.6 %gather_fusion.2 = bf16[128,128,128]{2,1,0:T(8,128)(2,1)} fusion(bf16[160,128,128]{2,1,0:T(8,128)(2,1)} %param.22, s32[1024]{0:T(1024)S(1)} %pad_clamp_fusion.1), kind=kCustom, calls=%fused_computation.2 | custom fusion | bytes 8389120 | tf_op jit(solution)/shard_map/gather | solution.py:243
  17.0 5.6 %gather_fusion.3 = bf16[128,128,128]{2,1,0:T(8,128)(2,1)} fusion(bf16[160,128,128]{2,1,0:T(8,128)(2,1)} %param.23, s32[1024]{0:T(1024)S(1)} %pad_clamp_fusion.1), kind=kCustom, calls=%fused_computation.3 | custom fusion | bytes 8389120 | tf_op jit(solution)/shard_map/gather | solution.py:244
  25.9 24.3 %all-gather.2.cloned.1.call-done = bf16[1024,2048]{1,0:T(8,128)(2,1)} async-done(((bf16[128,2048]{1,0:T(8,128)(2,1)}), bf16[1024,2048]{1,0:T(8,128)(2,1)}) %all-gather.2.cloned.1.call-update) | async-done | bytes 4194320 | tf_op jit(solution)/shard_map/all_gather | solution.py:218
  50.1 5.4 %fusion.141 = (bf16[1024,384]{1,0:T(8,128)(2,1)}, f32[1024,384]{1,0:T(8,128)S(1)}) fusion(bf16[1024,2048]{1,0:T(8,128)(2,1)} %all-gather.2.cloned.1.call-done, bf16[2048,128]{1,0:T(8,128)(2,1)S(1)} %get-tuple-element.283, bf16[2048,128]{1,0:T(8,128)(2,1)S(1)} %get-tuple-element.282, bf16[2048,128]{1,0:T(8,128)(2,1)S(1)} %copy-done.17), kind=kOutput, calls=%fused_computation.248 | convolution fusion | flops 1615724544 | bytes 8126464 | tf_op jit(solution)/shard_map/dot_general | solution.py:217
  60.3 2.8 fusion.14
  63.1 82.7 %while.18 = (s32[]{:T(128)}, f32[1020]{0:T(1024)S(1)}, f32[1020]{0:T(1024)S(1)}, f32[1020,128]{1,0:T(8,128)}, s32[]{:T(128)}, /*index=5*/s32[1,32]{1,0:T(1,128)S...) while((s32[]{:T(128)}, f32[1020]{0:T(1024)S(1)}, ...), condition=%wide.region_6.7_spmd.clone, body=%wide.region_3.6_spmd.clone.sunk | while | flops 273534432 | bytes 8434711 | solution.py:294
  63.2 3.1 gather_fusion
  67.9 3.1 gather_fusion.1
  72.6 3.1 gather_fusion
  77.3 3.1 gather_fusion.1
  83.1 3.1 gather_fusion
  87.8 3.1 gather_fusion.1
  93.6 3.1 gather_fusion
  98.3 3.1 gather_fusion.1
  104.0 3.1 gather_fusion
  108.7 3.1 gather_fusion.1
  114.5 3.1 gather_fusion
  119.2 3.1 gather_fusion.1
  125.0 3.1 gather_fusion
  129.7 3.1 gather_fusion.1
  135.4 3.1 gather_fusion
  140.2 3.1 gather_fusion.1
  145.8 3.0 fusion.94
  151.5 3.2 convolution_convert_fusion
  155.5 41.7 %all_gather.7 = f32[4096,16]{0,1:T(8,128)S(1)} all-gather(f32[128,16]{0,1:T(8,128)S(1)} %select_reduce_fusion.2), channel_id=1, replica_groups=mesh['req'=4,'exp'=8] {'req','exp'}, dimensions={0}, use_global_device_ids=true | all-gather | bytes 270336 | tf_op jit(solution)/shard_map/all_gather | solution.py:124
  197.4 11.5 %reduce-scatter.2.cloned.1.call-done = bf16[128,2048]{1,0:T(8,128)(2,1)} async-done(((bf16[1024,2048]{1,0:T(8,128)(2,1)}), bf16[128,2048]{1,0:T(8,128)(2,1)}) %reduce-scatter.2.cloned.1.call-update) | async-done | bytes 524304 | tf_op jit(solution)/shard_map/reduce_scatter | solution.py:300
  215.4 11.1 %collective-permute-done.32 = bf16[128,2048]{1,0:T(8,128)(2,1)S(1)} collective-permute-done((bf16[128,2048]{1,0:T(8,128)(2,1)S(1)}, bf16[128,2048]{1,0:T(8,128)(2,1)S(1)}, u32[]{:S(2)}, u32[]{:S(2)}) %collective-permute-start.32) | collective-permute-done | bytes 524320 | tf_op jit(solution)/shard_map/ppermute | solution.py:58
  230.2 3.2 collective-permute-done.34
  241.0 4.5 %fusion.145 = f32[512,1024]{1,0:T(8,128)S(1)} fusion(bf16[512,2048]{1,0:T(8,128)(2,1)S(1)} %constant_dynamic-update-slice_fusion.15, bf16[2048,1024]{1,0:T(8,128)(2,1)} %collective-permute-done.5), kind=kOutput, calls=%fused_computation.252 | convolution fusion | flops 2147483648 | bytes 8388608 | tf_op jit(solution)/shard_map/dot_general | solution.py:102
  245.5 2.9 multiply_convert_fusion
  255.0 3.5 collective-permute-done.38
  267.7 4.5 %fusion.142 = f32[512,1024]{1,0:T(8,128)S(1)} fusion(bf16[512,2048]{1,0:T(8,128)(2,1)S(1)} %constant_dynamic-update-slice_fusion, bf16[2048,1024]{1,0:T(8,128)(2,1)} %collective-permute-done.5), kind=kOutput, calls=%fused_computation.249 | convolution fusion | flops 2147483648 | bytes 8388608 | tf_op jit(solution)/shard_map/dot_general | solution.py:102
  272.3 2.9 multiply_convert_fusion.3
  277.4 5.8 %collective-permute-done.13 = bf16[128,2048]{1,0:T(8,128)(2,1)S(1)} collective-permute-done((bf16[128,2048]{1,0:T(8,128)(2,1)S(1)}, bf16[128,2048]{1,0:T(8,128)(2,1)S(1)}, u32[]{:S(2)}, u32[]{:S(2)}) %collective-permute-start.13) | collective-permute-done | bytes 524320 | tf_op jit(solution)/shard_map/ppermute | solution.py:58
  283.2 9.9 %collective-permute-start.22 = (bf16[128,2048]{1,0:T(8,128)(2,1)S(1)}, bf16[128,2048]{1,0:T(8,128)(2,1)S(1)}, u32[]{:S(2)}, u32[]{:S(2)}) collective-permute-start(bf16[128,2048]{1,0:T(8,128)(2,1)S(1)} %collective-permute-done.12), channel_id=1, source_target_pairs={{0,8},{8,16},{16,24},{24,0},{1,9},{9,17},{17,25},{25,1},{2,10},{10... | collective-permute-start | bytes 1572872 | tf_op jit(solution)/shard_map/ppermute | solution.py:63
  295.5 7.2 %collective-permute-done.22 = bf16[128,2048]{1,0:T(8,128)(2,1)S(1)} collective-permute-done((bf16[128,2048]{1,0:T(8,128)(2,1)S(1)}, bf16[128,2048]{1,0:T(8,128)(2,1)S(1)}, u32[]{:S(2)}, u32[]{:S(2)}) %collective-permute-start.22) | collective-permute-done | bytes 524320 | tf_op jit(solution)/shard_map/ppermute | solution.py:63
  308.5 4.5 %fusion.143 = f32[512,1024]{1,0:T(8,128)S(1)} fusion(bf16[512,2048]{1,0:T(8,128)(2,1)S(1)} %constant_dynamic-update-slice_fusion.5, bf16[2048,1024]{1,0:T(8,128)(2,1)} %collective-permute-done.5), kind=kOutput, calls=%fused_computation.250 | convolution fusion | flops 2147483648 | bytes 8388608 | tf_op jit(solution)/shard_map/dot_general | solution.py:102
  313.0 2.9 multiply_convert_fusion.2
  320.4 4.9 %collective-permute-done.17 = bf16[64,2048]{1,0:T(8,128)(2,1)S(1)} collective-permute-done((bf16[64,2048]{1,0:T(8,128)(2,1)S(1)}, bf16[64,2048]{1,0:T(8,128)(2,1)S(1)}, u32[]{:S(2)}, u32[]{:S(2)}) %collective-permute-start.17) | collective-permute-done | bytes 262176 | tf_op jit(solution)/shard_map/ppermute | solution.py:58
  327.6 8.1 %collective-permute-done.25 = bf16[64,2048]{1,0:T(8,128)(2,1)S(1)} collective-permute-done((bf16[64,2048]{1,0:T(8,128)(2,1)S(1)}, bf16[64,2048]{1,0:T(8,128)(2,1)S(1)}, u32[]{:S(2)}, u32[]{:S(2)}) %collective-permute-start.25) | collective-permute-done | bytes 262176 | tf_op jit(solution)/shard_map/ppermute | solution.py:58
  339.4 4.5 %fusion.144 = f32[512,1024]{1,0:T(8,128)S(1)} fusion(bf16[512,2048]{1,0:T(8,128)(2,1)S(1)} %constant_dynamic-update-slice_fusion.10, bf16[2048,1024]{1,0:T(8,128)(2,1)} %collective-permute-done.5), kind=kOutput, calls=%fused_computation.251 | convolution fusion | flops 2147483648 | bytes 8388608 | tf_op jit(solution)/shard_map/dot_general | solution.py:102
  343.9 3.1 multiply_convert_fusion.1
  349.3 7.1 %collective-permute-done.27 = bf16[64,2048]{1,0:T(8,128)(2,1)S(1)} collective-permute-done((bf16[64,2048]{1,0:T(8,128)(2,1)S(1)}, bf16[64,2048]{1,0:T(8,128)(2,1)S(1)}, u32[]{:S(2)}, u32[]{:S(2)}) %collective-permute-start.27) | collective-permute-done | bytes 262176 | tf_op jit(solution)/shard_map/ppermute | solution.py:58
  361.1 7.2 %collective-permute-done.18 = bf16[128,2048]{1,0:T(8,128)(2,1)S(1)} collective-permute-done((bf16[128,2048]{1,0:T(8,128)(2,1)S(1)}, bf16[128,2048]{1,0:T(8,128)(2,1)S(1)}, u32[]{:S(2)}, u32[]{:S(2)}) %collective-permute-start.18) | collective-permute-done | bytes 524320 | tf_op jit(solution)/shard_map/ppermute | solution.py:58
  368.6 3.4 collective-permute-done.20
  374.5 5.1 %collective-permute-done.30 = bf16[128,2048]{1,0:T(8,128)(2,1)S(1)} collective-permute-done((bf16[128,2048]{1,0:T(8,128)(2,1)S(1)}, bf16[128,2048]{1,0:T(8,128)(2,1)S(1)}, u32[]{:S(2)}, u32[]{:S(2)}) %collective-permute-start.30) | collective-permute-done | bytes 524320 | tf_op jit(solution)/shard_map/ppermute | solution.py:58
  380.9 4.3 %collective-permute-done.39 = bf16[128,2048]{1,0:T(8,128)(2,1)S(1)} collective-permute-done((bf16[128,2048]{1,0:T(8,128)(2,1)S(1)}, bf16[128,2048]{1,0:T(8,128)(2,1)S(1)}, u32[]{:S(2)}, u32[]{:S(2)}) %collective-permute-start.39) | collective-permute-done | bytes 524320 | tf_op jit(solution)/shard_map/ppermute | solution.py:58
  387.8 19.5 %collective-permute-done.21 = bf16[128,2048]{1,0:T(8,128)(2,1)S(1)} collective-permute-done((bf16[128,2048]{1,0:T(8,128)(2,1)S(1)}, bf16[128,2048]{1,0:T(8,128)(2,1)S(1)}, u32[]{:S(2)}, u32[]{:S(2)}) %collective-permute-start.21) | collective-permute-done | bytes 524320 | tf_op jit(solution)/shard_map/ppermute | solution.py:63
  (282 shorter events, 117.3 us)
Async XLA Ops:
  7.2 144.4 %copy-start = (bf16[128,2048]{1,0:T(8,128)(2,1)S(1)}, bf16[128,2048]{1,0:T(8,128)(2,1)}, u32[]{:S(2)}) copy-start(bf16[128,2048]{1,0:T(8,128)(2,1)} %param.28) | copy-start | bytes 1572868
  7.2 43.0 %all-gather.2.cloned.1.call-start = ((), (), s32[]{:S(2)}) async-start(), calls=%async_computation.1 | async-start | bytes 4718592 | tf_op jit(solution)/shard_map/all_gather | solution.py:218
  10.6 198.4 %reduce-scatter.2.cloned.1.call-start = ((), (), s32[]{:S(2)}) async-start(), calls=%async_computation.2 | async-start | bytes 4718592 | tf_op jit(solution)/shard_map/reduce_scatter | solution.py:300
  22.7 27.5 %copy-start.17 = (bf16[2048,128]{1,0:T(8,128)(2,1)S(1)}, bf16[2048,128]{1,0:T(8,128)(2,1)}, u32[]{:S(2)}) copy-start(bf16[2048,128]{1,0:T(8,128)(2,1)} %param.20) | copy-start | bytes 1572868
  154.7 54.2 %copy-start.3 = (bf16[128,2048]{1,0:T(8,128)(2,1)S(1)}, bf16[128,2048]{1,0:T(8,128)(2,1)}, u32[]{:S(2)}) copy-start(bf16[128,2048]{1,0:T(8,128)(2,1)} %param.18) | copy-start | bytes 1572868
  154.7 55.5 %copy-start.12 = (f32[2048]{0:T(1024)S(1)}, f32[2048]{0:T(1024)}, u32[]{:S(2)}) copy-start(f32[2048]{0:T(1024)} %param.29) | copy-start | bytes 24580
  154.8 86.2 %collective-permute-start.5 = (bf16[2048,1024]{1,0:T(8,128)(2,1)}, bf16[2048,1024]{1,0:T(8,128)(2,1)}, u32[]{:S(2)}, u32[]{:S(2)}) collective-permute-start(bf16[2048,1024]{1,0:T(8,128)(2,1)} %bitcast.130), channel_id=1, source_target_pairs={{0,1},{1,0},{2,3},{3,2},{4,5},{5,4},{6,7},{7,6},{8,9},{9,8},{10,11... | collective-permute-start | bytes 12582920 | tf_op jit(solution)/shard_map/ppermute | solution.py:58
  155.1 90.4 %collective-permute-start.6 = (bf16[512,2048]{1,0:T(8,128)(2,1)}, bf16[512,2048]{1,0:T(8,128)(2,1)}, u32[]{:S(2)}, u32[]{:S(2)}) collective-permute-start(bf16[512,2048]{1,0:T(8,128)(2,1)} %bitcast.131), channel_id=1, source_target_pairs={{0,1},{1,0},{2,3},{3,2},{4,5},{5,4},{6,7},{7,6},{8,9},{9,8},{10,11... | collective-permute-start | bytes 6291464 | tf_op jit(solution)/shard_map/ppermute | solution.py:58
  211.5 17.1 %collective-permute-start = (bf16[128,2048]{1,0:T(8,128)(2,1)S(1)}, bf16[128,2048]{1,0:T(8,128)(2,1)S(1)}, u32[]{:S(2)}, u32[]{:S(2)}) collective-permute-start(bf16[128,2048]{1,0:T(8,128)(2,1)S(1)} %get-tuple-element.247), channel_id=1, source_target_pairs={{0,8},{8,16},{16,24},{24,0},{1,9},{9,17},{17,25},{25,1},{2,10},{10... | collective-permute-start | bytes 1572872 | tf_op jit(solution)/shard_map/ppermute | solution.py:63
  213.1 13.4 %collective-permute-start.32 = (bf16[128,2048]{1,0:T(8,128)(2,1)S(1)}, bf16[128,2048]{1,0:T(8,128)(2,1)S(1)}, u32[]{:S(2)}, u32[]{:S(2)}) collective-permute-start(bf16[128,2048]{1,0:T(8,128)(2,1)S(1)} %get-tuple-element.247), channel_id=1, source_target_pairs={{0,2},{1,3},{2,0},{3,1},{4,6},{5,7},{6,4},{7,5},{8,10},{9,11},{10,... | collective-permute-start | bytes 1572872 | tf_op jit(solution)/shard_map/ppermute | solution.py:58
  214.5 13.4 %collective-permute-start.33 = (bf16[128,2048]{1,0:T(8,128)(2,1)S(1)}, bf16[128,2048]{1,0:T(8,128)(2,1)S(1)}, u32[]{:S(2)}, u32[]{:S(2)}) collective-permute-start(bf16[128,2048]{1,0:T(8,128)(2,1)S(1)} %get-tuple-element.247), channel_id=1, source_target_pairs={{0,4},{1,5},{2,6},{3,7},{4,0},{5,1},{6,2},{7,3},{8,12},{9,13},{10,... | collective-permute-start | bytes 1572872 | tf_op jit(solution)/shard_map/ppermute | solution.py:58
  226.5 6.9 %collective-permute-start.34 = (bf16[64,2048]{1,0:T(8,128)(2,1)S(1)}, bf16[64,2048]{1,0:T(8,128)(2,1)S(1)}, u32[]{:S(2)}, u32[]{:S(2)}) collective-permute-start(bf16[64,2048]{1,0:T(8,128)(2,1)S(1)} %slice.361), channel_id=1, source_target_pairs={{0,4},{1,5},{2,6},{3,7},{4,0},{5,1},{6,2},{7,3},{8,12},{9,13},{10,... | collective-permute-start | bytes 786440 | tf_op jit(solution)/shard_map/ppermute | solution.py:58
  228.0 9.3 %collective-permute-start.35 = (bf16[64,2048]{1,0:T(8,128)(2,1)S(1)}, bf16[64,2048]{1,0:T(8,128)(2,1)S(1)}, u32[]{:S(2)}, u32[]{:S(2)}) collective-permute-start(bf16[64,2048]{1,0:T(8,128)(2,1)S(1)} %slice.362), channel_id=1, source_target_pairs={{0,2},{1,3},{2,0},{3,1},{4,6},{5,7},{6,4},{7,5},{8,10},{9,11},{10,... | collective-permute-start | bytes 786440 | tf_op jit(solution)/shard_map/ppermute | solution.py:58
  228.7 23.5 %collective-permute-start.1 = (bf16[128,2048]{1,0:T(8,128)(2,1)S(1)}, bf16[128,2048]{1,0:T(8,128)(2,1)S(1)}, u32[]{:S(2)}, u32[]{:S(2)}) collective-permute-start(bf16[128,2048]{1,0:T(8,128)(2,1)S(1)} %collective-permute-done), channel_id=1, source_target_pairs={{0,2},{1,3},{2,0},{3,1},{4,6},{5,7},{6,4},{7,5},{8,10},{9,11},{10,... | collective-permute-start | bytes 1572872 | tf_op jit(solution)/shard_map/ppermute | solution.py:58
  233.4 19.5 %collective-permute-start.2 = (bf16[128,2048]{1,0:T(8,128)(2,1)S(1)}, bf16[128,2048]{1,0:T(8,128)(2,1)S(1)}, u32[]{:S(2)}, u32[]{:S(2)}) collective-permute-start(bf16[128,2048]{1,0:T(8,128)(2,1)S(1)} %collective-permute-done), channel_id=1, source_target_pairs={{0,4},{1,5},{2,6},{3,7},{4,0},{5,1},{6,2},{7,3},{8,12},{9,13},{10,... | collective-permute-start | bytes 1572872 | tf_op jit(solution)/shard_map/ppermute | solution.py:58
  248.5 6.4 %collective-permute-start.36 = (bf16[64,2048]{1,0:T(8,128)(2,1)S(1)}, bf16[64,2048]{1,0:T(8,128)(2,1)S(1)}, u32[]{:S(2)}, u32[]{:S(2)}) collective-permute-start(bf16[64,2048]{1,0:T(8,128)(2,1)S(1)} %get-tuple-element.277), channel_id=1, source_target_pairs={{0,4},{1,5},{2,6},{3,7},{4,0},{5,1},{6,2},{7,3},{8,12},{9,13},{10,... | collective-permute-start | bytes 786440 | tf_op jit(solution)/shard_map/ppermute | solution.py:58
  249.2 9.2 %collective-permute-start.38 = (bf16[64,2048]{1,0:T(8,128)(2,1)S(1)}, bf16[64,2048]{1,0:T(8,128)(2,1)S(1)}, u32[]{:S(2)}, u32[]{:S(2)}) collective-permute-start(bf16[64,2048]{1,0:T(8,128)(2,1)S(1)} %get-tuple-element.276), channel_id=1, source_target_pairs={{0,2},{1,3},{2,0},{3,1},{4,6},{5,7},{6,4},{7,5},{8,10},{9,11},{10,... | collective-permute-start | bytes 786440 | tf_op jit(solution)/shard_map/ppermute | solution.py:58
  250.7 11.0 %collective-permute-start.12 = (bf16[128,2048]{1,0:T(8,128)(2,1)S(1)}, bf16[128,2048]{1,0:T(8,128)(2,1)S(1)}, u32[]{:S(2)}, u32[]{:S(2)}) collective-permute-start(bf16[128,2048]{1,0:T(8,128)(2,1)S(1)} %collective-permute-done), channel_id=1, source_target_pairs={{0,8},{8,16},{16,24},{24,0},{1,9},{9,17},{17,25},{25,1},{2,10},{10... | collective-permute-start | bytes 1572872 | tf_op jit(solution)/shard_map/ppermute | solution.py:63
  252.2 11.5 %collective-permute-start.3 = (bf16[64,2048]{1,0:T(8,128)(2,1)S(1)}, bf16[64,2048]{1,0:T(8,128)(2,1)S(1)}, u32[]{:S(2)}, u32[]{:S(2)}) collective-permute-start(bf16[64,2048]{1,0:T(8,128)(2,1)S(1)} %slice.322), channel_id=1, source_target_pairs={{0,4},{1,5},{2,6},{3,7},{4,0},{5,1},{6,2},{7,3},{8,12},{9,13},{10,... | collective-permute-start | bytes 786440 | tf_op jit(solution)/shard_map/ppermute | solution.py:58
  252.9 11.2 %collective-permute-start.4 = (bf16[64,2048]{1,0:T(8,128)(2,1)S(1)}, bf16[64,2048]{1,0:T(8,128)(2,1)S(1)}, u32[]{:S(2)}, u32[]{:S(2)}) collective-permute-start(bf16[64,2048]{1,0:T(8,128)(2,1)S(1)} %slice.323), channel_id=1, source_target_pairs={{0,2},{1,3},{2,0},{3,1},{4,6},{5,7},{6,4},{7,5},{8,10},{9,11},{10,... | collective-permute-start | bytes 786440 | tf_op jit(solution)/shard_map/ppermute | solution.py:58
  258.7 122.3 %collective-permute-start.37 = (bf16[128,2048]{1,0:T(8,128)(2,1)S(1)}, bf16[128,2048]{1,0:T(8,128)(2,1)S(1)}, u32[]{:S(2)}, u32[]{:S(2)}) collective-permute-start(bf16[128,2048]{1,0:T(8,128)(2,1)S(1)} %pad_maximum_fusion.6), channel_id=1, source_target_pairs={{0,2},{1,3},{2,0},{3,1},{4,6},{5,7},{6,4},{7,5},{8,10},{9,11},{10,... | collective-permute-start | bytes 1572872 | tf_op jit(solution)/shard_map/ppermute | solution.py:58
  261.6 21.6 %collective-permute-start.13 = (bf16[128,2048]{1,0:T(8,128)(2,1)S(1)}, bf16[128,2048]{1,0:T(8,128)(2,1)S(1)}, u32[]{:S(2)}, u32[]{:S(2)}) collective-permute-start(bf16[128,2048]{1,0:T(8,128)(2,1)S(1)} %collective-permute-done.12), channel_id=1, source_target_pairs={{0,2},{1,3},{2,0},{3,1},{4,6},{5,7},{6,4},{7,5},{8,10},{9,11},{10,... | collective-permute-start | bytes 1572872 | tf_op jit(solution)/shard_map/ppermute | solution.py:58
  262.2 30.9 %collective-permute-start.14 = (bf16[128,2048]{1,0:T(8,128)(2,1)S(1)}, bf16[128,2048]{1,0:T(8,128)(2,1)S(1)}, u32[]{:S(2)}, u32[]{:S(2)}) collective-permute-start(bf16[128,2048]{1,0:T(8,128)(2,1)S(1)} %collective-permute-done.12), channel_id=1, source_target_pairs={{0,4},{1,5},{2,6},{3,7},{4,0},{5,1},{6,2},{7,3},{8,12},{9,13},{10,... | collective-permute-start | bytes 1572872 | tf_op jit(solution)/shard_map/ppermute | solution.py:58
  275.2 19.4 %collective-permute-start.7 = (bf16[64,2048]{1,0:T(8,128)(2,1)S(1)}, bf16[64,2048]{1,0:T(8,128)(2,1)S(1)}, u32[]{:S(2)}, u32[]{:S(2)}) collective-permute-start(bf16[64,2048]{1,0:T(8,128)(2,1)S(1)} %get-tuple-element.259), channel_id=1, source_target_pairs={{0,4},{1,5},{2,6},{3,7},{4,0},{5,1},{6,2},{7,3},{8,12},{9,13},{10,... | collective-permute-start | bytes 786440 | tf_op jit(solution)/shard_map/ppermute | solution.py:58
  276.7 18.6 %collective-permute-start.9 = (bf16[64,2048]{1,0:T(8,128)(2,1)S(1)}, bf16[64,2048]{1,0:T(8,128)(2,1)S(1)}, u32[]{:S(2)}, u32[]{:S(2)}) collective-permute-start(bf16[64,2048]{1,0:T(8,128)(2,1)S(1)} %get-tuple-element.258), channel_id=1, source_target_pairs={{0,2},{1,3},{2,0},{3,1},{4,6},{5,7},{6,4},{7,5},{8,10},{9,11},{10,... | collective-permute-start | bytes 786440 | tf_op jit(solution)/shard_map/ppermute | solution.py:58
  283.2 19.5 %collective-permute-start.22 = (bf16[128,2048]{1,0:T(8,128)(2,1)S(1)}, bf16[128,2048]{1,0:T(8,128)(2,1)S(1)}, u32[]{:S(2)}, u32[]{:S(2)}) collective-permute-start(bf16[128,2048]{1,0:T(8,128)(2,1)S(1)} %collective-permute-done.12), channel_id=1, source_target_pairs={{0,8},{8,16},{16,24},{24,0},{1,9},{9,17},{17,25},{25,1},{2,10},{10... | collective-permute-start | bytes 1572872 | tf_op jit(solution)/shard_map/ppermute | solution.py:63
  293.2 11.6 %collective-permute-start.15 = (bf16[64,2048]{1,0:T(8,128)(2,1)S(1)}, bf16[64,2048]{1,0:T(8,128)(2,1)S(1)}, u32[]{:S(2)}, u32[]{:S(2)}) collective-permute-start(bf16[64,2048]{1,0:T(8,128)(2,1)S(1)} %slice.335), channel_id=1, source_target_pairs={{0,4},{1,5},{2,6},{3,7},{4,0},{5,1},{6,2},{7,3},{8,12},{9,13},{10,... | collective-permute-start | bytes 786440 | tf_op jit(solution)/shard_map/ppermute | solution.py:58
  294.7 10.1 %collective-permute-start.16 = (bf16[64,2048]{1,0:T(8,128)(2,1)S(1)}, bf16[64,2048]{1,0:T(8,128)(2,1)S(1)}, u32[]{:S(2)}, u32[]{:S(2)}) collective-permute-start(bf16[64,2048]{1,0:T(8,128)(2,1)S(1)} %slice.336), channel_id=1, source_target_pairs={{0,2},{1,3},{2,0},{3,1},{4,6},{5,7},{6,4},{7,5},{8,10},{9,11},{10,... | collective-permute-start | bytes 786440 | tf_op jit(solution)/shard_map/ppermute | solution.py:58
  302.7 15.6 %collective-permute-start.23 = (bf16[128,2048]{1,0:T(8,128)(2,1)S(1)}, bf16[128,2048]{1,0:T(8,128)(2,1)S(1)}, u32[]{:S(2)}, u32[]{:S(2)}) collective-permute-start(bf16[128,2048]{1,0:T(8,128)(2,1)S(1)} %collective-permute-done.22), channel_id=1, source_target_pairs={{0,2},{1,3},{2,0},{3,1},{4,6},{5,7},{6,4},{7,5},{8,10},{9,11},{10,... | collective-permute-start | bytes 1572872 | tf_op jit(solution)/shard_map/ppermute | solution.py:58
  304.0 15.7 %collective-permute-start.24 = (bf16[128,2048]{1,0:T(8,128)(2,1)S(1)}, bf16[128,2048]{1,0:T(8,128)(2,1)S(1)}, u32[]{:S(2)}, u32[]{:S(2)}) collective-permute-start(bf16[128,2048]{1,0:T(8,128)(2,1)S(1)} %collective-permute-done.22), channel_id=1, source_target_pairs={{0,4},{1,5},{2,6},{3,7},{4,0},{5,1},{6,2},{7,3},{8,12},{9,13},{10,... | collective-permute-start | bytes 1572872 | tf_op jit(solution)/shard_map/ppermute | solution.py:58
  316.0 9.3 %collective-permute-start.17 = (bf16[64,2048]{1,0:T(8,128)(2,1)S(1)}, bf16[64,2048]{1,0:T(8,128)(2,1)S(1)}, u32[]{:S(2)}, u32[]{:S(2)}) collective-permute-start(bf16[64,2048]{1,0:T(8,128)(2,1)S(1)} %get-tuple-element.265), channel_id=1, source_target_pairs={{0,4},{1,5},{2,6},{3,7},{4,0},{5,1},{6,2},{7,3},{8,12},{9,13},{10,... | collective-permute-start | bytes 786440 | tf_op jit(solution)/shard_map/ppermute | solution.py:58
  317.5 9.2 %collective-permute-start.19 = (bf16[64,2048]{1,0:T(8,128)(2,1)S(1)}, bf16[64,2048]{1,0:T(8,128)(2,1)S(1)}, u32[]{:S(2)}, u32[]{:S(2)}) collective-permute-start(bf16[64,2048]{1,0:T(8,128)(2,1)S(1)} %get-tuple-element.264), channel_id=1, source_target_pairs={{0,2},{1,3},{2,0},{3,1},{4,6},{5,7},{6,4},{7,5},{8,10},{9,11},{10,... | collective-permute-start | bytes 786440 | tf_op jit(solution)/shard_map/ppermute | solution.py:58
  318.2 40.5 %collective-permute-start.8 = (bf16[128,2048]{1,0:T(8,128)(2,1)S(1)}, bf16[128,2048]{1,0:T(8,128)(2,1)S(1)}, u32[]{:S(2)}, u32[]{:S(2)}) collective-permute-start(bf16[128,2048]{1,0:T(8,128)(2,1)S(1)} %pad_maximum_fusion), channel_id=1, source_target_pairs={{0,2},{1,3},{2,0},{3,1},{4,6},{5,7},{6,4},{7,5},{8,10},{9,11},{10,... | collective-permute-start | bytes 1572872 | tf_op jit(solution)/shard_map/ppermute | solution.py:58
  319.7 39.8 %collective-permute-start.10 = (bf16[128,2048]{1,0:T(8,128)(2,1)S(1)}, bf16[128,2048]{1,0:T(8,128)(2,1)S(1)}, u32[]{:S(2)}, u32[]{:S(2)}) collective-permute-start(bf16[128,2048]{1,0:T(8,128)(2,1)S(1)} %pad_maximum_fusion.1), channel_id=1, source_target_pairs={{0,4},{1,5},{2,6},{3,7},{4,0},{5,1},{6,2},{7,3},{8,12},{9,13},{10,... | collective-permute-start | bytes 1572872 | tf_op jit(solution)/shard_map/ppermute | solution.py:58
  325.3 10.4 %collective-permute-start.25 = (bf16[64,2048]{1,0:T(8,128)(2,1)S(1)}, bf16[64,2048]{1,0:T(8,128)(2,1)S(1)}, u32[]{:S(2)}, u32[]{:S(2)}) collective-permute-start(bf16[64,2048]{1,0:T(8,128)(2,1)S(1)} %slice.348), channel_id=1, source_target_pairs={{0,4},{1,5},{2,6},{3,7},{4,0},{5,1},{6,2},{7,3},{8,12},{9,13},{10,... | collective-permute-start | bytes 786440 | tf_op jit(solution)/shard_map/ppermute | solution.py:58
  326.7 9.0 %collective-permute-start.26 = (bf16[64,2048]{1,0:T(8,128)(2,1)S(1)}, bf16[64,2048]{1,0:T(8,128)(2,1)S(1)}, u32[]{:S(2)}, u32[]{:S(2)}) collective-permute-start(bf16[64,2048]{1,0:T(8,128)(2,1)S(1)} %slice.349), channel_id=1, source_target_pairs={{0,2},{1,3},{2,0},{3,1},{4,6},{5,7},{6,4},{7,5},{8,10},{9,11},{10,... | collective-permute-start | bytes 786440 | tf_op jit(solution)/shard_map/ppermute | solution.py:58
  347.1 9.3 %collective-permute-start.27 = (bf16[64,2048]{1,0:T(8,128)(2,1)S(1)}, bf16[64,2048]{1,0:T(8,128)(2,1)S(1)}, u32[]{:S(2)}, u32[]{:S(2)}) collective-permute-start(bf16[64,2048]{1,0:T(8,128)(2,1)S(1)} %get-tuple-element.271), channel_id=1, source_target_pairs={{0,4},{1,5},{2,6},{3,7},{4,0},{5,1},{6,2},{7,3},{8,12},{9,13},{10,... | collective-permute-start | bytes 786440 | tf_op jit(solution)/shard_map/ppermute | solution.py:58
  347.8 9.2 %collective-permute-start.29 = (bf16[64,2048]{1,0:T(8,128)(2,1)S(1)}, bf16[64,2048]{1,0:T(8,128)(2,1)S(1)}, u32[]{:S(2)}, u32[]{:S(2)}) collective-permute-start(bf16[64,2048]{1,0:T(8,128)(2,1)S(1)} %get-tuple-element.270), channel_id=1, source_target_pairs={{0,2},{1,3},{2,0},{3,1},{4,6},{5,7},{6,4},{7,5},{8,10},{9,11},{10,... | collective-permute-start | bytes 786440 | tf_op jit(solution)/shard_map/ppermute | solution.py:58
  356.5 11.8 %collective-permute-start.18 = (bf16[128,2048]{1,0:T(8,128)(2,1)S(1)}, bf16[128,2048]{1,0:T(8,128)(2,1)S(1)}, u32[]{:S(2)}, u32[]{:S(2)}) collective-permute-start(bf16[128,2048]{1,0:T(8,128)(2,1)S(1)} %pad_maximum_fusion.2), channel_id=1, source_target_pairs={{0,2},{1,3},{2,0},{3,1},{4,6},{5,7},{6,4},{7,5},{8,10},{9,11},{10,... | collective-permute-start | bytes 1572872 | tf_op jit(solution)/shard_map/ppermute | solution.py:58
  357.1 14.9 %collective-permute-start.20 = (bf16[128,2048]{1,0:T(8,128)(2,1)S(1)}, bf16[128,2048]{1,0:T(8,128)(2,1)S(1)}, u32[]{:S(2)}, u32[]{:S(2)}) collective-permute-start(bf16[128,2048]{1,0:T(8,128)(2,1)S(1)} %pad_maximum_fusion.3), channel_id=1, source_target_pairs={{0,4},{1,5},{2,6},{3,7},{4,0},{5,1},{6,2},{7,3},{8,12},{9,13},{10,... | collective-permute-start | bytes 1572872 | tf_op jit(solution)/shard_map/ppermute | solution.py:58
  358.7 15.2 %collective-permute-start.28 = (bf16[128,2048]{1,0:T(8,128)(2,1)S(1)}, bf16[128,2048]{1,0:T(8,128)(2,1)S(1)}, u32[]{:S(2)}, u32[]{:S(2)}) collective-permute-start(bf16[128,2048]{1,0:T(8,128)(2,1)S(1)} %pad_maximum_fusion.4), channel_id=1, source_target_pairs={{0,2},{1,3},{2,0},{3,1},{4,6},{5,7},{6,4},{7,5},{8,10},{9,11},{10,... | collective-permute-start | bytes 1572872 | tf_op jit(solution)/shard_map/ppermute | solution.py:58
  359.4 20.2 %collective-permute-start.30 = (bf16[128,2048]{1,0:T(8,128)(2,1)S(1)}, bf16[128,2048]{1,0:T(8,128)(2,1)S(1)}, u32[]{:S(2)}, u32[]{:S(2)}) collective-permute-start(bf16[128,2048]{1,0:T(8,128)(2,1)S(1)} %pad_maximum_fusion.5), channel_id=1, source_target_pairs={{0,4},{1,5},{2,6},{3,7},{4,0},{5,1},{6,2},{7,3},{8,12},{9,13},{10,... | collective-permute-start | bytes 1572872 | tf_op jit(solution)/shard_map/ppermute | solution.py:58
  368.3 16.9 %collective-permute-start.39 = (bf16[128,2048]{1,0:T(8,128)(2,1)S(1)}, bf16[128,2048]{1,0:T(8,128)(2,1)S(1)}, u32[]{:S(2)}, u32[]{:S(2)}) collective-permute-start(bf16[128,2048]{1,0:T(8,128)(2,1)S(1)} %pad_maximum_fusion.7), channel_id=1, source_target_pairs={{0,4},{1,5},{2,6},{3,7},{4,0},{5,1},{6,2},{7,3},{8,12},{9,13},{10,... | collective-permute-start | bytes 1572872 | tf_op jit(solution)/shard_map/ppermute | solution.py:58
  371.9 15.9 %collective-permute-start.11 = (bf16[128,2048]{1,0:T(8,128)(2,1)S(1)}, bf16[128,2048]{1,0:T(8,128)(2,1)S(1)}, u32[]{:S(2)}, u32[]{:S(2)}) collective-permute-start(bf16[128,2048]{1,0:T(8,128)(2,1)S(1)} %add_convert_fusion.2), channel_id=1, source_target_pairs={{0,24},{8,0},{16,8},{24,16},{1,25},{9,1},{17,9},{25,17},{2,26},{10... | collective-permute-start | bytes 1572872 | tf_op jit(solution)/shard_map/ppermute | solution.py:63
  372.7 34.6 %copy-start.4 = (bf16[128,2048]{1,0:T(8,128)(2,1)S(1)}, bf16[128,2048]{1,0:T(8,128)(2,1)}, u32[]{:S(2)}) copy-start(bf16[128,2048]{1,0:T(8,128)(2,1)} %reduce-scatter.2.cloned.1.call-done) | copy-start | bytes 1572868
  373.9 33.4 %collective-permute-start.21 = (bf16[128,2048]{1,0:T(8,128)(2,1)S(1)}, bf16[128,2048]{1,0:T(8,128)(2,1)S(1)}, u32[]{:S(2)}, u32[]{:S(2)}) collective-permute-start(bf16[128,2048]{1,0:T(8,128)(2,1)S(1)} %add_convert_fusion.1), channel_id=1, source_target_pairs={{0,16},{8,24},{16,0},{24,8},{1,17},{9,25},{17,1},{25,9},{2,18},{10... | collective-permute-start | bytes 1572872 | tf_op jit(solution)/shard_map/ppermute | solution.py:63
  379.9 27.5 %collective-permute-start.31 = (bf16[128,2048]{1,0:T(8,128)(2,1)S(1)}, bf16[128,2048]{1,0:T(8,128)(2,1)S(1)}, u32[]{:S(2)}, u32[]{:S(2)}) collective-permute-start(bf16[128,2048]{1,0:T(8,128)(2,1)S(1)} %add_convert_fusion), channel_id=1, source_target_pairs={{0,8},{8,16},{16,24},{24,0},{1,9},{9,17},{17,25},{25,1},{2,10},{10... | collective-permute-start | bytes 1572872 | tf_op jit(solution)/shard_map/ppermute | solution.py:63
  380.0 28.9 %copy-start.1 = (bf16[128,2048]{1,0:T(8,128)(2,1)S(1)}, bf16[128,2048]{1,0:T(8,128)(2,1)}, u32[]{:S(2)}) copy-start(bf16[128,2048]{1,0:T(8,128)(2,1)} %param.28) | copy-start | bytes 1572868
  (14 other events, 76.9 us)
Sparse Core Ops, SparseCore 0:
  10.7 39.4 all-gather.1
  154.9 54.0 reduce-scatter.1
